TPU v7x, 32 devices: a whole 2x2x4 slice. The times are simulated.
32 devices in a mesh: rows: 8 (over z, x), batch: 4 (over y, core).
Axes of the slice: x: 2, y: 2, z: 4, core: 2. Of those that a mesh axis runs over, the one named last changes fastest.
Arguments:
- features: bfloat16 [4, 64, 128, 256], P('batch', 'rows'), may hold values from -6 to 6
- kernels: bfloat16 [3, 3, 3, 256, 256], replicated, may hold values from -0.125 to 0.125
- cotangent: bfloat16 [4, 64, 128, 256], P('batch', 'rows'), may hold values from -6 to 6
Outputs:
- result: bfloat16 [4, 64, 128, 256], P('batch', 'rows')
- grad_features: bfloat16 [4, 64, 128, 256], P('batch', 'rows')
- grad_kernels: float32 [3, 3, 3, 256, 256], replicated
All inputs are finite; a program needn't handle non-finite values.
Results may differ from a plain program's by a relative error of at most 0.0065.
Values may be sent and summed in bfloat16 or wider, within the bound.
A program may use at most 128 MiB of HBM per device.

v0:
```python
import math

import jax
import jax.numpy as jnp
from jax import lax
from jax.sharding import PartitionSpec as P


def passed_along(value, axis, steps):
    count = lax.axis_size(axis)
    initial, last = (max(0, -steps), min(count, count - steps))
    return lax.ppermute(value, axis, [(source, source + steps) for source in range(initial, last)])


def activate(values):
    values = values.astype(jnp.float32)
    normed = values * lax.rsqrt(jnp.mean(values * values, axis=-1, keepdims=True) + 1e-05)
    return normed * jax.nn.sigmoid(normed)


def shift_columns(array, offset):
    width = array.shape[2]
    reach = abs(offset)
    padded = jnp.pad(array, ((0, 0), (0, 0), (reach, reach), (0, 0)))
    return padded[:, :, reach + offset : reach + offset + width]


def tap_forward(source, kernel_row, dilation):
    channels = kernel_row.shape[1]
    widened = jnp.transpose(kernel_row, (1, 0, 2)).reshape(channels, 3 * channels)
    product = jnp.einsum("shwc,cd->shwd", source, widened, preferred_element_type=jnp.float32)
    total = shift_columns(product[..., 0:channels], -dilation)
    total = total + product[..., channels : 2 * channels]
    return total + shift_columns(product[..., 2 * channels :], dilation)


def tap_backward(source, kernel_row, dilation):
    channels = kernel_row.shape[1]
    widened = jnp.transpose(kernel_row, (2, 0, 1)).reshape(channels, 3 * channels)
    product = jnp.einsum("shwd,dc->shwc", source, widened, preferred_element_type=jnp.float32)
    total = shift_columns(product[..., 0:channels], dilation)
    total = total + product[..., channels : 2 * channels]
    return total + shift_columns(product[..., 2 * channels :], -dilation)


def kernel_terms(source, grad_flow, dilation):
    channels = grad_flow.shape[3]
    stacked = jnp.concatenate(
        [shift_columns(grad_flow, dilation), grad_flow, shift_columns(grad_flow, -dilation)], axis=3
    )
    terms = jnp.einsum("shwc,shwd->cd", source, stacked, preferred_element_type=jnp.float32)
    return jnp.transpose(terms.reshape(channels, 3, channels), (1, 0, 2))


def fetch_bands(signal, bands_away):
    upper_band = passed_along(signal, "rows", bands_away)
    lower_band = passed_along(signal, "rows", -bands_away)
    return (upper_band, lower_band)


def fetch_grads(grad_flow, bands_away):
    grad_upper = passed_along(grad_flow, "rows", bands_away)
    grad_lower = passed_along(grad_flow, "rows", -bands_away)
    return (grad_upper, grad_lower)


def local(features, kernels, cotangent):
    band_rows = features.shape[1]
    count = lax.axis_size("rows")
    spans = [4, 8, 16]
    current = features
    grad_flow = cotangent
    saved = []
    for layer in range(3):
        dilation = spans[layer] * band_rows
        signal = activate(current).astype(jnp.bfloat16)
        upper_band, lower_band = fetch_bands(signal, spans[layer])
        conv_out = tap_forward(signal, kernels[layer, 1], dilation)
        conv_out = conv_out + tap_forward(upper_band, kernels[layer, 0], dilation)
        conv_out = conv_out + tap_forward(lower_band, kernels[layer, 2], dilation)
        saved.append((current, signal, upper_band, lower_band))
        current = (current.astype(jnp.float32) + conv_out).astype(jnp.bfloat16)
    pixel_count = features.shape[0] * band_rows * features.shape[2] * count * lax.axis_size("batch")
    factor = 1.0 / math.sqrt(pixel_count)
    kernel_grads = [None, None, None]
    for layer in [2, 1, 0]:
        dilation = spans[layer] * band_rows
        layer_input, signal, upper_band, lower_band = saved[layer]
        grad_upper, grad_lower = fetch_grads(grad_flow, spans[layer])
        dsignal = tap_backward(grad_flow, kernels[layer, 1], dilation)
        dsignal = dsignal + tap_backward(grad_lower, kernels[layer, 0], dilation)
        dsignal = dsignal + tap_backward(grad_upper, kernels[layer, 2], dilation)
        local_grad = (
            jnp.stack(
                [
                    kernel_terms(upper_band, grad_flow, dilation),
                    kernel_terms(signal, grad_flow, dilation),
                    kernel_terms(lower_band, grad_flow, dilation),
                ]
            )
            * factor
        )
        kernel_grads[layer] = lax.psum(local_grad, ("rows", "batch"))
        _, back = jax.vjp(activate, layer_input.astype(jnp.float32))
        (dinput,) = back(dsignal)
        grad_flow = (grad_flow.astype(jnp.float32) + dinput).astype(jnp.bfloat16)
    summed = jnp.stack(kernel_grads)
    return (current, grad_flow, summed)


def solution(mesh):
    placed = (P("batch", "rows", None, None), P(), P("batch", "rows", None, None))
    return jax.shard_map(
        local,
        mesh=mesh,
        in_specs=placed,
        out_specs=(P("batch", "rows", None, None), P("batch", "rows", None, None), P()),
        check_vma=False,
    )
```

profile of v0, /device:TPU:0, one launch (start us, length us, event | category | flops | bytes accessed | tf_op | source)
XLA Modules:
  0.0 298.2 jit_solution(7352963170528896677)
XLA Ops:
  7.2 1.3 fusion.75
  8.5 2.2 fusion.50
  10.7 1.3 collective-permute-start.1
  12.0 7.6 %collective-permute-start = (bf16[1,8,128,256]{3,2,1,0:T(8,128)(2,1)}, bf16[1,8,128,256]{3,2,1,0:T(8,128)(2,1)}, u32[]{:S(2)}, u32[]{:S(2)}) collective-permute-start(bf16[1,8,128,256]{3,2,1,0:T(8,128)(2,1)} %fusion.50), channel_id=1, source_target_pairs={{0,16},{4,20},{8,24},{12,28},{1,17},{5,21},{9,25},{13,29},{2,18},{... | collective-permute-start | bytes 1572872 | tf_op jit(solution)/shard_map/ppermute | solution.py:12
  19.5 1.5 collective-permute-start.4
  21.0 3.5 %fusion.133 = (bf16[1,1,3,256,256]{4,3,2,1,0:T(8,128)(2,1)}, bf16[1,1,3,256,256]{4,3,2,1,0:T(8,128)(2,1)}, bf16[1,1,3,256,256]{4,3,2,1,0:T(8,128)(2,1)}, bf16[1,...) fusion(bf16[3,3,3,256,256]{4,3,2,1,0:T(8,128)(2,1)} %param.4), kind=kLoop, calls=%fused_computation.207 | loop fusion | bytes 7077888 | tf_op jit(solution)/shard_map/slice | solution.py:78
  25.4 1.8 convolution_bitcast_fusion.17
  27.3 2.6 convolution_bitcast_fusion.8
  29.9 2.1 copy.84
  32.1 1.5 fusion.143
  33.7 1.3 pad_maximum_fusion.1
  38.2 1.2 collective-permute-done.1
  39.4 1.6 convolution_bitcast_fusion.15
  41.3 1.6 convolution_bitcast_fusion.16
  44.7 1.8 fusion.77
  48.2 1.7 convolution_bitcast_fusion.6
  50.0 1.7 convolution_bitcast_fusion.7
  54.8 2.1 fusion.90
  56.9 1.4 fusion.62
  58.3 1.5 collective-permute-start.5
  59.9 1.5 collective-permute-start.3
  61.4 2.5 fusion.29
  63.9 1.3 maximum_bitcast_fusion.1
  65.2 3.0 copy.79
  68.2 2.2 fusion.23
  71.0 1.6 fusion.1
  74.2 1.6 convolution_bitcast_fusion.3
  76.9 1.6 convolution_bitcast_fusion.4
  80.3 1.3 maximum_bitcast_fusion
  81.5 2.9 copy.72
  84.4 2.3 convolution_bitcast_fusion.19
  86.8 1.7 fusion.26
  88.5 1.6 fusion.2
  90.5 1.7 convolution_bitcast_fusion.18
  92.2 1.7 convolution_bitcast_fusion.20
  93.9 1.6 fusion
  95.5 2.0 copy.154
  99.3 1.8 convolution_bitcast_fusion.11
  101.1 1.4 collective-permute-start.7
  102.5 1.5 collective-permute-start.6
  105.7 1.7 convolution_bitcast_fusion.9
  107.3 1.6 convolution_bitcast_fusion.10
  109.0 1.1 fusion.89
  110.1 14.3 %collective-permute-done.7 = bf16[1,8,128,256]{3,2,1,0:T(8,128)(2,1)S(1)} collective-permute-done((bf16[1,8,128,256]{3,2,1,0:T(8,128)(2,1)S(1)}, bf16[1,8,128,256]{3,2,1,0:T(8,128)(2,1)S(1)}, u32[]{:S(2)}, u32[]{:S(2)}) %collective-permute-start.7) | collective-permute-done | bytes 524320 | tf_op jit(solution)/shard_map/ppermute | solution.py:12
  125.0 16.8 %collective-permute-done.6 = bf16[1,8,128,256]{3,2,1,0:T(8,128)(2,1)S(1)} collective-permute-done((bf16[1,8,128,256]{3,2,1,0:T(8,128)(2,1)S(1)}, bf16[1,8,128,256]{3,2,1,0:T(8,128)(2,1)S(1)}, u32[]{:S(2)}, u32[]{:S(2)}) %collective-permute-start.6) | collective-permute-done | bytes 524320 | tf_op jit(solution)/shard_map/ppermute | solution.py:12
  144.0 1.2 fusion.74
  145.2 139.4 %all-reduce.29.cloned.1.call-done = (f32[1,3,3,256,256]{4,3,2,1,0:T(8,128)}, f32[1,3,3,256,256]{4,3,2,1,0:T(8,128)}, f32[1,3,3,256,256]{4,3,2,1,0:T(8,128)}) async-done(((f32[1,3,3,256,256]{4,3,2,1,0:T(8,128)}, f32[1,3,3,256,256]{4,3,2,1,0:T(8,128)}, f32[1,3,3,256,256]{4,3,2,1,0:T(8,128)}), (f32[1,3,3,256,256]{4,3,2,1,0:T(8,128)}, f32[1,3,3,256,256]{4,3,2,1,0:T(8,128)}, ...) | async-done | bytes 7077904 | tf_op jit(solution)/shard_map/psum | solution.py:103
  284.5 6.8 %pad_maximum_fusion = f32[3,3,3,256,256]{4,3,2,1,0:T(8,128)} fusion(f32[1,3,3,256,256]{4,3,2,1,0:T(8,128)} %get-tuple-element.3, f32[1,3,3,256,256]{4,3,2,1,0:T(8,128)} %get-tuple-element.4, f32[1,3,3,256,256]{4,3,2,1,0:T(8,128)} %get-tuple-element.5), kind=kLoop, calls=%fused_computation | loop fusion | flops 3538944 | bytes 14155776 | tf_op jit(solution)/shard_map/stack | solution.py:107
  (118 shorter events, 22.4 us)
Async XLA Ops:
  7.2 277.4 %all-reduce.29.cloned.1.call-start = ((), (), s32[]{:S(2)}) async-start(), calls=%async_computation | async-start | bytes 14155776 | tf_op jit(solution)/shard_map/psum | solution.py:103
  10.7 28.8 %collective-permute-start.1 = (bf16[1,8,128,256]{3,2,1,0:T(8,128)(2,1)}, bf16[1,8,128,256]{3,2,1,0:T(8,128)(2,1)}, u32[]{:S(2)}, u32[]{:S(2)}) collective-permute-start(bf16[1,8,128,256]{3,2,1,0:T(8,128)(2,1)} %fusion.50), channel_id=1, source_target_pairs={{16,0},{20,4},{24,8},{28,12},{17,1},{21,5},{25,9},{29,13},{18,2},{... | collective-permute-start | bytes 1572872 | tf_op jit(solution)/shard_map/ppermute | solution.py:12
  12.0 29.3 %collective-permute-start = (bf16[1,8,128,256]{3,2,1,0:T(8,128)(2,1)}, bf16[1,8,128,256]{3,2,1,0:T(8,128)(2,1)}, u32[]{:S(2)}, u32[]{:S(2)}) collective-permute-start(bf16[1,8,128,256]{3,2,1,0:T(8,128)(2,1)} %fusion.50), channel_id=1, source_target_pairs={{0,16},{4,20},{8,24},{12,28},{1,17},{5,21},{9,25},{13,29},{2,18},{... | collective-permute-start | bytes 1572872 | tf_op jit(solution)/shard_map/ppermute | solution.py:12
  19.5 28.7 %collective-permute-start.4 = (bf16[1,8,128,256]{3,2,1,0:T(8,128)(2,1)}, bf16[1,8,128,256]{3,2,1,0:T(8,128)(2,1)}, u32[]{:S(2)}, u32[]{:S(2)}) collective-permute-start(bf16[1,8,128,256]{3,2,1,0:T(8,128)(2,1)} %param.5), channel_id=1, source_target_pairs={} | collective-permute-start | bytes 1572872 | tf_op jit(solution)/shard_map/ppermute | solution.py:12
  24.5 0.9 copy-start.7
  25.4 1.9 copy-start.2
  25.4 1.9 copy-start.9
  27.2 4.8 %copy-start.1 = (f32[1,8,128,768]{3,2,1,0:T(8,128)}, f32[1,8,128,768]{3,2,1,0:T(8,128)S(1)}, u32[]{:S(2)}) copy-start(f32[1,8,128,768]{3,2,1,0:T(8,128)S(1)} %convolution_bitcast_fusion.17) | copy-start | bytes 9437188
  32.1 1.6 copy-start.20
  33.6 1.4 copy-start.14
  33.6 2.4 copy-start.6
  33.7 2.6 copy-start.16
  33.7 3.6 %copy-start.18 = (bf16[1,1,3,256,256]{4,3,2,1,0:T(8,128)(2,1)S(1)}, bf16[1,1,3,256,256]{4,3,2,1,0:T(8,128)(2,1)}, u32[]{:S(2)}) copy-start(bf16[1,1,3,256,256]{4,3,2,1,0:T(8,128)(2,1)} %get-tuple-element.20) | copy-start | bytes 1179652
  42.9 1.0 copy-start
  43.0 1.4 copy-start.4
  43.0 1.7 copy-start.5
  44.7 2.9 copy-start.31
  46.5 1.7 copy-start.13
  46.9 3.1 %copy-start.21 = (bf16[1,8,128,256]{3,2,1,0:T(8,128)(2,1)}, bf16[1,8,128,256]{3,2,1,0:T(8,128)(2,1)S(1)}, u32[]{:S(2)}) copy-start(bf16[1,8,128,256]{3,2,1,0:T(8,128)(2,1)S(1)} %fusion.44) | copy-start | bytes 1572868
  46.9 4.9 %collective-permute-start.2 = (bf16[1,8,128,256]{3,2,1,0:T(8,128)(2,1)S(1)}, bf16[1,8,128,256]{3,2,1,0:T(8,128)(2,1)S(1)}, u32[]{:S(2)}, u32[]{:S(2)}) collective-permute-start(bf16[1,8,128,256]{3,2,1,0:T(8,128)(2,1)S(1)} %fusion.44), channel_id=1, source_target_pairs={} | collective-permute-start | bytes 1572872 | tf_op jit(solution)/shard_map/ppermute | solution.py:12
  48.2 1.7 copy-start.11
  51.6 1.0 copy-start.29
  51.8 1.5 copy-start.30
  51.8 1.4 copy-start.23
  54.8 2.1 copy-start.3
  56.9 4.4 %copy-start.25 = (bf16[1,8,128,768]{2,1,3,0:T(8,128)(2,1)S(1)}, bf16[1,8,128,768]{2,1,3,0:T(8,128)(2,1)}, u32[]{:S(2)}) copy-start(bf16[1,8,128,768]{2,1,3,0:T(8,128)(2,1)} %pad_maximum_fusion.1) | copy-start | bytes 4718596
  58.3 15.1 %collective-permute-start.5 = (bf16[1,8,128,256]{3,2,1,0:T(8,128)(2,1)S(1)}, bf16[1,8,128,256]{3,2,1,0:T(8,128)(2,1)}, u32[]{:S(2)}, u32[]{:S(2)}) collective-permute-start(bf16[1,8,128,256]{3,2,1,0:T(8,128)(2,1)S(1)} %get-tuple-element.49), channel_id=1, source_target_pairs={} | collective-permute-start | bytes 1572872 | tf_op jit(solution)/shard_map/ppermute | solution.py:12
  59.9 26.9 %collective-permute-start.3 = (bf16[1,8,128,256]{3,2,1,0:T(8,128)(2,1)}, bf16[1,8,128,256]{3,2,1,0:T(8,128)(2,1)}, u32[]{:S(2)}, u32[]{:S(2)}) collective-permute-start(bf16[1,8,128,256]{3,2,1,0:T(8,128)(2,1)} %get-tuple-element.50), channel_id=1, source_target_pairs={} | collective-permute-start | bytes 1572872 | tf_op jit(solution)/shard_map/ppermute | solution.py:12
  65.2 3.0 %copy-start.22 = (bf16[1,8,128,256]{3,2,1,0:T(8,128)(2,1)S(1)}, bf16[1,8,128,256]{3,2,1,0:T(8,128)(2,1)}, u32[]{:S(2)}) copy-start(bf16[1,8,128,256]{3,2,1,0:T(8,128)(2,1)} %copy-done.21) | copy-start | bytes 1572868
  68.1 2.2 copy-start.24
  68.1 2.2 copy-start.28
  71.0 1.6 copy-start.19
  73.2 1.0 copy-start.17
  75.9 1.0 copy-start.15
  84.4 2.3 copy-start.26
  86.8 1.8 copy-start.34
  88.5 2.0 copy-start.27
  95.5 2.0 copy-start.12
  95.5 2.9 copy-start.10
  98.4 5.6 %copy-start.8 = (bf16[1,1,3,256,256]{4,3,2,1,0:T(8,128)(2,1)S(1)}, bf16[1,1,3,256,256]{4,3,2,1,0:T(8,128)(2,1)}, u32[]{:S(2)}) copy-start(bf16[1,1,3,256,256]{4,3,2,1,0:T(8,128)(2,1)} %copy-done.7) | copy-start | bytes 1179652
  101.1 23.3 %collective-permute-start.7 = (bf16[1,8,128,256]{3,2,1,0:T(8,128)(2,1)S(1)}, bf16[1,8,128,256]{3,2,1,0:T(8,128)(2,1)S(1)}, u32[]{:S(2)}, u32[]{:S(2)}) collective-permute-start(bf16[1,8,128,256]{3,2,1,0:T(8,128)(2,1)S(1)} %fusion.64), channel_id=1, source_target_pairs={{0,16},{4,20},{8,24},{12,28},{1,17},{5,21},{9,25},{13,29},{2,18},{... | collective-permute-start | bytes 1572872 | tf_op jit(solution)/shard_map/ppermute | solution.py:12
  102.5 39.3 %collective-permute-start.6 = (bf16[1,8,128,256]{3,2,1,0:T(8,128)(2,1)S(1)}, bf16[1,8,128,256]{3,2,1,0:T(8,128)(2,1)S(1)}, u32[]{:S(2)}, u32[]{:S(2)}) collective-permute-start(bf16[1,8,128,256]{3,2,1,0:T(8,128)(2,1)S(1)} %fusion.64), channel_id=1, source_target_pairs={{16,0},{20,4},{24,8},{28,12},{17,1},{21,5},{25,9},{29,13},{18,2},{... | collective-permute-start | bytes 1572872 | tf_op jit(solution)/shard_map/ppermute | solution.py:12
  104.7 1.0 copy-start.33
  104.9 2.5 copy-start.32
Sparse Core Ops, SparseCore 0:
  95.6 188.8 all-reduce.28
where the time goes:
time: 299 us; the launch traced here: 298 us
  waiting for transfers between devices  172 us (58%)
  matrix products  36.4 us (12%)
  other arithmetic  30 us (10%)
  local copies, waits for them, and re-layouts  28.4 us (9%)
  starting transfers between devices  17 us (6%)
  between operations  14.7 us (5%)
    psum x1, waiting for transfers between devices, local(): kernel_grads[layer] = lax.psum(local_grad, ('rows', 'batch'))  139 us
    ppermute x8, waiting for transfers between devices, passed_along(): lax.ppermute(value, axis, [(source, source + steps) for source in range(i...  32.4 us
    ppermute x8, starting transfers between devices, passed_along(): lax.ppermute(value, axis, [(source, source + steps) for source in range(i...  16.9 us
    unnamed x80, local copies, waits for them, and re-layouts  15.2 us
    dot_general x7, matrix products, kernel_terms(): jnp.einsum('shwc,shwd->cd', source, stacked, preferred_element_type=jnp.f...  12.7 us
    dot_general x9, matrix products, tap_forward(): jnp.einsum('shwc,cd->shwd', source, widened, preferred_element_type=jnp.f...  12 us
    dot_general x9, matrix products, tap_backward(): jnp.einsum('shwd,dc->shwc', source, widened, preferred_element_type=jnp.f...  11.7 us
    another operation x4, other arithmetic, local(): summed = jnp.stack(kernel_grads)  11.6 us
  transfers between devices with their start and end apart: 9, of which 4 were waited for; matrix products, arithmetic and copies ran while one was open for 22% of the time, Pallas kernels for 0%

commit v1 on v0

v1 whole, which is shorter than its diff:
```python
import math

import jax
import jax.numpy as jnp
from jax import lax
from jax.sharding import PartitionSpec as P


def passed_along(value, axis, steps):
    count = lax.axis_size(axis)
    initial, last = (max(0, -steps), min(count, count - steps))
    return lax.ppermute(value, axis, [(source, source + steps) for source in range(initial, last)])


def swapped(value, axis, steps):
    count = lax.axis_size(axis)
    return lax.ppermute(value, axis, [(source, (source + steps) % count) for source in range(count)])


def activate(values):
    values = values.astype(jnp.float32)
    normed = values * lax.rsqrt(jnp.mean(values * values, axis=-1, keepdims=True) + 1e-05)
    return normed * jax.nn.sigmoid(normed)


def shift_columns(array, offset):
    width = array.shape[2]
    reach = abs(offset)
    padded = jnp.pad(array, ((0, 0), (0, 0), (reach, reach), (0, 0)))
    return padded[:, :, reach + offset : reach + offset + width]


def column_taps(width, dilation):
    return [0, 1, 2] if dilation < width else [1]


def tap_forward(source, kernel_row, dilation):
    total = 0.0
    for column in column_taps(source.shape[2], dilation):
        product = jnp.einsum(
            "shwc,cd->shwd", source, kernel_row[column], preferred_element_type=jnp.float32
        )
        total = total + shift_columns(product, (column - 1) * dilation)
    return total


def tap_backward(source, kernel_row, dilation):
    total = 0.0
    for column in column_taps(source.shape[2], dilation):
        product = jnp.einsum(
            "shwd,cd->shwc", source, kernel_row[column], preferred_element_type=jnp.float32
        )
        total = total + shift_columns(product, (1 - column) * dilation)
    return total


def kernel_terms(source, grad_flow, dilation):
    terms = []
    for column in column_taps(source.shape[2], dilation):
        terms.append(
            jnp.einsum(
                "shwc,shwd->cd",
                source,
                shift_columns(grad_flow, (1 - column) * dilation),
                preferred_element_type=jnp.float32,
            )
        )
    return jnp.stack(terms)


def fetch(value, span):
    count = lax.axis_size("rows")
    if span >= count:
        return []
    if 2 * span == count:
        return [(None, swapped(value, "rows", span))]
    return [(0, passed_along(value, "rows", span)), (2, passed_along(value, "rows", -span))]


def local(features, kernels, cotangent):
    band_rows, width = features.shape[1:3]
    count = lax.axis_size("rows")
    spans = [4, 8, 16]
    below = lax.axis_index("rows")
    current = features
    grad_flow = cotangent
    saved = []
    for layer in range(3):
        dilation = spans[layer] * band_rows
        is_lower = below >= spans[layer]
        signal = activate(current).astype(jnp.bfloat16)
        bands = fetch(signal, spans[layer])
        conv_out = tap_forward(signal, kernels[layer, 1], dilation)
        for row, band in bands:
            weights = (
                jnp.where(is_lower, kernels[layer, 0], kernels[layer, 2])
                if row is None
                else kernels[layer, row]
            )
            conv_out = conv_out + tap_forward(band, weights, dilation)
        saved.append((current, signal, bands))
        current = (current.astype(jnp.float32) + conv_out).astype(jnp.bfloat16)
    pixel_count = features.shape[0] * band_rows * width * count * lax.axis_size("batch")
    factor = 1.0 / math.sqrt(pixel_count)
    kernel_grads = [None, None, None]
    for layer in [2, 1, 0]:
        dilation = spans[layer] * band_rows
        is_lower = below >= spans[layer]
        layer_input, signal, bands = saved[layer]
        terms = {1: kernel_terms(signal, grad_flow, dilation)}
        for row, band in bands:
            term = kernel_terms(band, grad_flow, dilation)
            if row is None:
                terms[0] = jnp.where(is_lower, term, 0.0)
                terms[2] = jnp.where(is_lower, 0.0, term)
            else:
                terms[row] = term
        stacked = jnp.stack([terms[row] for row in sorted(terms)]) * factor
        stacked = lax.psum(stacked, ("rows", "batch"))
        wide_r, wide_c = (3 - stacked.shape[0]) // 2, (3 - stacked.shape[1]) // 2
        kernel_grads[layer] = jnp.pad(
            stacked, ((wide_r, wide_r), (wide_c, wide_c), (0, 0), (0, 0))
        )
        dsignal = tap_backward(grad_flow, kernels[layer, 1], dilation)
        for row, band in fetch(grad_flow, spans[layer]):
            weights = (
                jnp.where(is_lower, kernels[layer, 2], kernels[layer, 0])
                if row is None
                else kernels[layer, 2 - row]
            )
            dsignal = dsignal + tap_backward(band, weights, dilation)
        _, back = jax.vjp(activate, layer_input.astype(jnp.float32))
        (dinput,) = back(dsignal)
        grad_flow = (grad_flow.astype(jnp.float32) + dinput).astype(jnp.bfloat16)
    return (current, grad_flow, jnp.stack(kernel_grads))


def solution(mesh):
    placed = (P("batch", "rows", None, None), P(), P("batch", "rows", None, None))
    return jax.shard_map(
        local,
        mesh=mesh,
        in_specs=placed,
        out_specs=(P("batch", "rows", None, None), P("batch", "rows", None, None), P()),
        check_vma=False,
    )
```

time: 299 us -> 218 us (0.73)
  local copies, waits for them, and re-layouts: 28.4 us -> 1.99 us
  other arithmetic: 30 us -> 12.3 us
  waiting for transfers between devices: 172 us -> 156 us
  starting transfers between devices: 17 us -> 4.21 us
  matrix products: 36.4 us -> 28.8 us
    psum x1, waiting for transfers between devices: 139 us -> 116 us  [local(): stacked = lax.psum(stacked, ('rows', 'batch'))]
    unnamed x80 -> x10, local copies, waits for them, and re-layouts: 15.2 us -> 0.22 us
    ppermute x8 -> x2, starting transfers between devices: 16.9 us -> 4.17 us  [swapped(): lax.ppermute(value, axis, [(source, (source + steps) % count) for source...]
    dot_general x25 -> x30, matrix products: 36.4 us -> 28.8 us  [the longest x10 12.4 us: tap_backward(): jnp.einsum('shwd,cd->shwc', source, kernel_row[column], preferred_element...]
    ppermute x8 -> x2, waiting for transfers between devices: 32.4 us -> 39.9 us  [swapped(): lax.ppermute(value, axis, [(source, (source + steps) % count) for source...]
    slice x15 -> x0, local copies, waits for them, and re-layouts: 7.26 us -> none  [the longest x1 3.46 us: local(): conv_out = tap_forward(signal, kernels[layer, 1], dilation)]
    another operation x4, other arithmetic: 11.6 us -> 5.46 us  [the longest x2 5.03 us: local(): return (current, grad_flow, jnp.stack(kernel_grads))]
    dot_general x2 -> x0, local copies, waits for them, and re-layouts: 5.9 us -> none  [kernel_terms(): jnp.einsum('shwc,shwd->cd', source, stacked, preferred_element_type=jnp.f...]
  transfers between devices with their start and end apart: 9 -> 3, of which waited for: 4 -> 3; matrix products, arithmetic and copies ran while one was open for 22% -> 9% of each run, Pallas kernels for 0% -> 0%
where the time goes in v1:
time: 218 us
  waiting for transfers between devices  156 us (72%)
  matrix products  28.8 us (13%)
  between operations  14.3 us (7%)
  other arithmetic  12.3 us (6%)
  starting transfers between devices  4.21 us (2%)
    psum x1, waiting for transfers between devices, local(): stacked = lax.psum(stacked, ('rows', 'batch'))  116 us
    ppermute x2, waiting for transfers between devices, swapped(): lax.ppermute(value, axis, [(source, (source + steps) % count) for source...  39.9 us
    dot_general x10, matrix products, tap_backward(): jnp.einsum('shwd,cd->shwc', source, kernel_row[column], preferred_element...  12.4 us
    dot_general x10, matrix products, tap_forward(): jnp.einsum('shwc,cd->shwd', source, kernel_row[column], preferred_element...  12 us
    another operation x2, other arithmetic, local(): return (current, grad_flow, jnp.stack(kernel_grads))  5.03 us
    dot_general x10, matrix products, kernel_terms(): jnp.einsum('shwc,shwd->cd', source, shift_columns(grad_flow, (1 - column)...  4.38 us
  transfers between devices with their start and end apart: 3, of which 3 were waited for; matrix products, arithmetic and copies ran while one was open for 9% of the time, Pallas kernels for 0%

profile of v1, /device:TPU:0, one launch (start us, length us, event | category | flops | bytes accessed | tf_op | source)
XLA Modules:
  0.0 217.6 jit_solution(1234145157922967561)
XLA Ops:
  7.2 1.3 fusion.52
  8.5 1.4 fusion.37
  9.9 4.1 %collective-permute-start = (bf16[1,8,128,256]{3,2,1,0:T(8,128)(2,1)S(1)}, bf16[1,8,128,256]{3,2,1,0:T(8,128)(2,1)S(1)}, u32[]{:S(2)}, u32[]{:S(2)}) collective-permute-start(bf16[1,8,128,256]{3,2,1,0:T(8,128)(2,1)S(1)} %fusion.37), channel_id=1, source_target_pairs={{0,16},{4,20},{8,24},{12,28},{16,0},{20,4},{24,8},{28,12},{1,17},{... | collective-permute-start | bytes 1572872 | tf_op jit(solution)/shard_map/ppermute | solution.py:17
  14.0 1.2 convolution_bitcast_fusion.17
  15.2 2.2 convolution_bitcast_fusion.19
  17.4 1.2 broadcast_select_fusion
  18.5 1.6 fusion.11
  20.1 17.0 %collective-permute-done = bf16[1,8,128,256]{3,2,1,0:T(8,128)(2,1)S(1)} collective-permute-done((bf16[1,8,128,256]{3,2,1,0:T(8,128)(2,1)S(1)}, bf16[1,8,128,256]{3,2,1,0:T(8,128)(2,1)S(1)}, u32[]{:S(2)}, u32[]{:S(2)}) %collective-permute-start) | collective-permute-done | bytes 524320 | tf_op jit(solution)/shard_map/ppermute | solution.py:17
  37.1 0.3 convolution_bitcast_fusion.14
  37.4 0.3 convolution_bitcast_fusion.16
  37.8 0.5 fusion.55
  38.3 0.4 fusion.63
  38.7 1.3 convolution_bitcast_fusion.11
  39.9 1.2 convolution_bitcast_fusion.13
  41.1 1.3 fusion.57
  42.5 1.3 fusion.21
  43.9 1.6 fusion.58
  45.5 0.4 fusion.44
  45.9 0.3 convolution_bitcast_fusion.22
  46.2 0.3 convolution_bitcast_fusion.21
  46.6 0.3 convolution_bitcast_fusion.23
  46.9 1.2 convolution_bitcast_fusion.6
  48.2 1.2 convolution_bitcast_fusion.8
  49.4 1.7 fusion.56
  51.1 0.4 fusion.46
  51.5 0.3 convolution_bitcast_fusion.26
  51.8 0.3 convolution_bitcast_fusion.24
  52.2 0.3 convolution_bitcast_fusion.25
  52.5 0.1 collective-permute-start.1
  52.6 1.2 convolution_bitcast_fusion.3
  53.8 2.2 %convolution_bitcast_fusion.5 = f32[1,8,128,256]{3,2,1,0:T(8,128)} fusion(bf16[1,8,128,256]{3,2,1,0:T(8,128)(2,1)S(1)} %fusion.46, bf16[3,3,3,256,256]{4,3,2,1,0:T(8,128)(2,1)} %param.4), kind=kOutput, calls=%fused_computation.52 | convolution fusion | flops 134217728 | bytes 1703936 | tf_op jit(solution)/shard_map/shwd,cd->shwc/dot_general | solution.py:50
  56.0 0.9 maximum_multiply_fusion.1
  57.1 0.3 convolution_bitcast_fusion.28
  57.4 0.3 convolution_bitcast_fusion.27
  57.7 0.3 convolution_bitcast_fusion.29
  58.1 0.1 fusion.60
  58.2 1.6 fusion
  59.9 1.6 fusion.17
  61.5 2.2 %fusion.18 = bf16[1,8,128,256]{3,2,1,0:T(8,128)(2,1)} fusion(bf16[1,8,128,256]{3,2,1,0:T(8,128)(2,1)S(1)} %copy-done.3, bf16[3,3,3,256,256]{4,3,2,1,0:T(8,128)(2,1)} %param.4, f32[8,128]{1,0:T(8,128)S(1)} %fusion.133), kind=kOutput, calls=%fused_computation.75 | convolution fusion | flops 136839168 | bytes 1708032 | tf_op jit(solution)/shard_map/shwc,cd->shwd/dot_general | solution.py:40
  63.7 22.9 %collective-permute-done.1 = bf16[1,8,128,256]{3,2,1,0:T(8,128)(2,1)S(1)} collective-permute-done((bf16[1,8,128,256]{3,2,1,0:T(8,128)(2,1)S(1)}, bf16[1,8,128,256]{3,2,1,0:T(8,128)(2,1)S(1)}, u32[]{:S(2)}, u32[]{:S(2)}) %collective-permute-start.1) | collective-permute-done | bytes 524320 | tf_op jit(solution)/shard_map/ppermute | solution.py:17
  86.6 0.3 convolution_bitcast_fusion
  86.9 0.3 convolution_bitcast_fusion.2
  87.2 0.9 fusion.54
  88.2 1.1 fusion.51
  89.3 116.0 %all-reduce.19.cloned.1.call-done = (f32[1,1,256,256]{3,2,1,0:T(8,128)}, f32[1,3,256,256]{3,2,1,0:T(8,128)}, f32[1,3,3,256,256]{4,3,2,1,0:T(8,128)}) async-done(((f32[1,1,256,256]{3,2,1,0:T(8,128)}, f32[1,3,256,256]{3,2,1,0:T(8,128)}, f32[1,3,3,256,256]{4,3,2,1,0:T(8,128)}), (f32[1,1,256,256]{3,2,1,0:T(8,128)}, f32[1,3,256,256]{3,2,1,0:T(8,128)}, ...) | async-done | bytes 3407888 | tf_op jit(solution)/shard_map/psum | solution.py:119
  205.3 1.8 pad_bitcast_fusion
  207.1 0.2 copy-done.1
  207.3 3.4 %pad_maximum_fusion = f32[3,3,3,256,256]{4,3,2,1,0:T(8,128)} fusion(f32[1,3,3,256,256]{4,3,2,1,0:T(8,128)S(1)} %get-tuple-element.20, f32[1,3,3,256,256]{4,3,2,1,0:T(8,128)S(1)} %get-tuple-element.21, f32[1,3,3,256,256]{4,3,2,1,0:T(8,128)S(1)} %copy-done.1), kind=kLoop, calls=%fused_computation | loop fusion | flops 3538944 | bytes 14155776 | tf_op jit(solution)/shard_map/stack | solution.py:135
  (18 shorter events, 0.2 us)
Async XLA Ops:
  7.2 198.2 %all-reduce.19.cloned.1.call-start = ((), (), s32[]{:S(2)}) async-start(), calls=%async_computation | async-start | bytes 6815744 | tf_op jit(solution)/shard_map/psum | solution.py:119
  9.9 27.3 %collective-permute-start = (bf16[1,8,128,256]{3,2,1,0:T(8,128)(2,1)S(1)}, bf16[1,8,128,256]{3,2,1,0:T(8,128)(2,1)S(1)}, u32[]{:S(2)}, u32[]{:S(2)}) collective-permute-start(bf16[1,8,128,256]{3,2,1,0:T(8,128)(2,1)S(1)} %fusion.37), channel_id=1, source_target_pairs={{0,16},{4,20},{8,24},{12,28},{16,0},{20,4},{24,8},{28,12},{1,17},{... | collective-permute-start | bytes 1572872 | tf_op jit(solution)/shard_map/ppermute | solution.py:17
  18.5 19.2 %copy-start = (bf16[1,8,128,256]{3,2,1,0:T(8,128)(2,1)S(1)}, bf16[1,8,128,256]{3,2,1,0:T(8,128)(2,1)}, u32[]{:S(2)}) copy-start(bf16[1,8,128,256]{3,2,1,0:T(8,128)(2,1)} %param.3) | copy-start | bytes 1572868
  38.7 3.9 %copy-start.4 = (bf16[1,8,128,256]{3,2,1,0:T(8,128)(2,1)S(1)}, bf16[1,8,128,256]{3,2,1,0:T(8,128)(2,1)}, u32[]{:S(2)}) copy-start(bf16[1,8,128,256]{3,2,1,0:T(8,128)(2,1)} %param.5) | copy-start | bytes 1572868
  42.5 3.0 %copy-start.2 = (bf16[1,8,128,256]{3,2,1,0:T(8,128)(2,1)}, bf16[1,8,128,256]{3,2,1,0:T(8,128)(2,1)S(1)}, u32[]{:S(2)}) copy-start(bf16[1,8,128,256]{3,2,1,0:T(8,128)(2,1)S(1)} %get-tuple-element.13) | copy-start | bytes 1572868
  52.5 34.1 %collective-permute-start.1 = (bf16[1,8,128,256]{3,2,1,0:T(8,128)(2,1)S(1)}, bf16[1,8,128,256]{3,2,1,0:T(8,128)(2,1)S(1)}, u32[]{:S(2)}, u32[]{:S(2)}) collective-permute-start(bf16[1,8,128,256]{3,2,1,0:T(8,128)(2,1)S(1)} %fusion.46), channel_id=1, source_target_pairs={{0,16},{4,20},{8,24},{12,28},{16,0},{20,4},{24,8},{28,12},{1,17},{... | collective-permute-start | bytes 1572872 | tf_op jit(solution)/shard_map/ppermute | solution.py:17
  59.8 1.6 copy-start.3
  205.3 2.0 copy-start.1
Sparse Core Ops, SparseCore 0:
  60.0 145.2 all-reduce.18

commit v2 on v1

--- a/solution.py
+++ b/solution.py
@@ -1,9 +1,14 @@
+import functools
 import math
 
 import jax
 import jax.numpy as jnp
 from jax import lax
+from jax.experimental import pallas as pl
+from jax.experimental.pallas import tpu as pltpu
 from jax.sharding import PartitionSpec as P
+
+SPANS = (4, 8, 16)
 
 
 def passed_along(value, axis, steps):
@@ -80,7 +85,7 @@
 def local(features, kernels, cotangent):
     band_rows, width = features.shape[1:3]
     count = lax.axis_size("rows")
-    spans = [4, 8, 16]
+    spans = SPANS
     below = lax.axis_index("rows")
     current = features
     grad_flow = cotangent
@@ -135,10 +140,407 @@
     return (current, grad_flow, jnp.stack(kernel_grads))
 
 
+MESH = pl.DeviceIdType.MESH
+CHUNKS = 4
+FLAT = (((1,), (0,)), ((), ()))
+TURNED = (((1,), (1,)), ((), ()))
+SUMMED = (((0,), (0,)), ((), ()))
+
+
+def normalise(values):
+    scale = lax.rsqrt(jnp.mean(values * values, axis=-1, keepdims=True) + 1e-05)
+    normed = values * scale
+    gate = 1.0 / (1.0 + jnp.exp(-normed))
+    return scale, normed, gate
+
+
+def activate_back(values, dsignal):
+    scale, normed, gate = normalise(values)
+    dnormed = dsignal * (gate + normed * gate * (1.0 - gate))
+    return scale * (dnormed - normed * jnp.mean(dnormed * normed, axis=-1, keepdims=True))
+
+
+def moved(array, offset):
+    if offset == 0:
+        return array
+    blank = jnp.zeros((array.shape[0], abs(offset), array.shape[2]), array.dtype)
+    if offset > 0:
+        return jnp.concatenate([array[:, offset:], blank], axis=1)
+    return jnp.concatenate([blank, array[:, :offset]], axis=1)
+
+
+def flat(array):
+    return array.reshape(array.shape[0] * array.shape[1], array.shape[2])
+
+
+def fused_kernel(
+    dilations, features, kernels, cotangent, result, grad_features, gathered,
+    weights, signal0, other0, signal1, signal2, flow2, flow1, other1, center, center1,
+    parts, from_core, core_sum, from_plane, sum_common, sum_side, from_line, from_side,
+    load_sem, swap_send, swap_recv, core_send, core_recv, plane_send, plane_recv,
+    line_send, line_recv, side_send, side_recv, gline_send, gline_recv,
+    gplane_send, gplane_recv, gcore_send, gcore_recv,
+):
+    band_rows, width, channels = features.shape
+    step = band_rows // CHUNKS
+    near, mid = dilations[0], dilations[1]
+    row, batch = lax.axis_index("rows"), lax.axis_index("batch")
+    line, across = lax.div(row, 2), lax.rem(row, 2)
+    plane_y, core = lax.div(batch, 2), lax.rem(batch, 2)
+    member = plane_y * 2 + across
+    lower = lax.div(line, 2)
+    side = lax.rem(line, 2)
+
+    def toggled(value, bits):
+        if bits == 1:
+            return value + 1 - 2 * lax.rem(value, 2)
+        if bits == 2:
+            return lax.rem(value + 2, 4)
+        return 3 - value
+
+    def on_line(bits):
+        return (toggled(line, bits) * 2 + across, batch)
+
+    def on_plane(bits):
+        other = toggled(member, bits)
+        return (line * 2 + lax.rem(other, 2), lax.div(other, 2) * 2 + core)
+
+    core_mate = (row, plane_y * 2 + 1 - core)
+    swap_mate = on_line(2)
+
+    loads = []
+    first = 0
+    for slot, (tap, taps) in enumerate(((0, 9), (12, 3), (22, 1))):
+        copy = pltpu.make_async_copy(
+            kernels.at[pl.ds(tap * channels, taps * channels)],
+            weights.at[pl.ds(first * channels, taps * channels)],
+            load_sem.at[slot],
+        )
+        copy.start()
+        loads.append(copy)
+        first += taps
+
+    barrier = pltpu.get_barrier_semaphore()
+    mates = [core_mate] + [on_line(k) for k in (1, 2, 3)] + [on_plane(k) for k in (1, 2, 3)]
+    for mate in mates:
+        pl.semaphore_signal(barrier, inc=1, device_id=mate, device_id_type=MESH)
+    pl.semaphore_wait(barrier, len(mates))
+
+    def remote(source, target, send, recv, mate):
+        return pltpu.make_async_remote_copy(
+            src_ref=source, dst_ref=target, send_sem=send, recv_sem=recv,
+            device_id=mate, device_id_type=MESH,
+        )
+
+    def swap_signal(k):
+        rows = pl.ds(k * step, step)
+        return remote(
+            signal0.at[rows], other0.at[rows], swap_send.at[k], swap_recv.at[k], swap_mate
+        )
+
+    def swap_flow(k):
+        rows = pl.ds(k * step, step)
+        return remote(
+            flow1.at[rows], other1.at[rows],
+            swap_send.at[CHUNKS + k], swap_recv.at[CHUNKS + k], swap_mate,
+        )
+
+    def dot(left, right, how):
+        return lax.dot_general(left, right, how, preferred_element_type=jnp.float32)
+
+    def wide(start):
+        if isinstance(start, int):
+            return weights[start * channels : (start + 3) * channels]
+        return weights[pl.ds(pl.multiple_of(start * channels, channels), 3 * channels)]
+
+    def forward(array, start, dilation):
+        return dot(
+            jnp.concatenate(
+                [flat(moved(array, -dilation)), flat(array), flat(moved(array, dilation))], axis=1
+            ),
+            wide(start),
+            FLAT,
+        )
+
+    def backward(array, start, dilation):
+        taps = wide(start)
+        total = dot(flat(array), taps[channels : 2 * channels], TURNED)
+        total = total + dot(flat(moved(array, dilation)), taps[:channels], TURNED)
+        return total + dot(flat(moved(array, -dilation)), taps[2 * channels :], TURNED)
+
+    def each_chunk(body):
+        def run(k, carry):
+            body(k)
+            return carry
+
+        lax.fori_loop(0, CHUNKS, run, 0)
+
+    def send_signal(k):
+        rows = pl.ds(k * step, step)
+        values = flat(features[rows].astype(jnp.float32))
+        _, normed, gate = normalise(values)
+        signal0[rows] = (normed * gate).astype(jnp.bfloat16).reshape(step, width, channels)
+        swap_signal(k).start()
+
+    each_chunk(send_signal)
+    loads[0].wait()
+
+    def own_forward(k):
+        rows = pl.ds(k * step, step)
+        total = forward(signal0[rows], 3, near)
+        center[rows] = (flat(features[rows].astype(jnp.float32)) + total).reshape(
+            step, width, channels
+        )
+
+    each_chunk(own_forward)
+    loads[1].wait()
+    loads[2].wait()
+
+    def through(k):
+        rows = pl.ds(k * step, step)
+        shape = (step, width, channels)
+        swap_signal(k).wait_recv()
+        upper = forward(other0[rows], (1 - lower) * 6, near)
+        inner = (flat(center[rows]) + upper).astype(jnp.bfloat16).astype(jnp.float32)
+        _, normed, gate = normalise(inner)
+        signal = (normed * gate).astype(jnp.bfloat16).reshape(shape)
+        signal1[rows] = signal
+        deep = (inner + forward(signal, 9, mid)).astype(jnp.bfloat16).astype(jnp.float32)
+        _, normed, gate = normalise(deep)
+        signal = (normed * gate).astype(jnp.bfloat16)
+        signal2[rows] = signal.reshape(shape)
+        last = weights[12 * channels : 13 * channels]
+        result[rows] = (deep + dot(signal, last, FLAT)).astype(jnp.bfloat16).reshape(shape)
+        flow = cotangent[rows]
+        dsignal = dot(flat(flow), last, TURNED)
+        flow = (flat(flow.astype(jnp.float32)) + activate_back(deep, dsignal)).astype(jnp.bfloat16)
+        flow = flow.reshape(shape)
+        flow2[rows] = flow
+        dsignal = backward(flow, 9, mid)
+        flow = flat(flow.astype(jnp.float32)) + activate_back(inner, dsignal)
+        flow1[rows] = flow.astype(jnp.bfloat16).reshape(shape)
+        swap_flow(k).start()
+
+    each_chunk(through)
+
+    def keep(tap, terms):
+        half, quarter = channels // 2, channels // 4
+        terms = terms.astype(jnp.bfloat16)
+        for h in range(2):
+            for q in range(4):
+                parts[h, q, tap] = terms[
+                    q * quarter : (q + 1) * quarter, h * half : (h + 1) * half
+                ]
+
+    def gradient(source, flow, dilation, tap):
+        if dilation is None:
+            keep(tap, dot(flat(source), flat(flow), SUMMED))
+            return
+        for c in range(3):
+            keep(tap + c, dot(flat(source), flat(moved(flow, (1 - c) * dilation)), SUMMED))
+
+    gradient(signal2[...], cotangent[...], None, 6)
+    gradient(signal1[...], flow2[...], mid, 3)
+    gradient(signal0[...], flow1[...], near, 0)
+    gradient(other0[...], flow1[...], near, 7)
+
+    to_core = remote(parts.at[1 - core], from_core, core_send, core_recv, core_mate)
+    to_core.start()
+
+    def own_backward(k):
+        rows = pl.ds(k * step, step)
+        center1[rows] = backward(flow1[rows], 3, near).reshape(step, width, channels)
+
+    each_chunk(own_backward)
+
+    def finish(k):
+        rows = pl.ds(k * step, step)
+        swap_flow(k).wait_recv()
+        dsignal = flat(center1[rows]) + backward(other1[rows], lower * 6, near)
+        flow = flat(flow1[rows].astype(jnp.float32))
+        flow = flow + activate_back(flat(features[rows].astype(jnp.float32)), dsignal)
+        grad_features[rows] = flow.astype(jnp.bfloat16).reshape(step, width, channels)
+
+    to_core.wait_recv()
+    core_sum[...] = (
+        parts[core].astype(jnp.float32) + from_core[...].astype(jnp.float32)
+    ).astype(jnp.bfloat16)
+    to_plane = []
+    for k in (1, 2, 3):
+        copy = remote(
+            core_sum.at[toggled(member, k)], from_plane.at[k - 1],
+            plane_send.at[k - 1], plane_recv.at[k - 1], on_plane(k),
+        )
+        copy.start()
+        to_plane.append(copy)
+
+    finish(0)
+    for copy in to_plane:
+        copy.wait_recv()
+    total = core_sum[member].astype(jnp.float32)
+    for k in range(3):
+        total = total + from_plane[k].astype(jnp.float32)
+    total = total.astype(jnp.bfloat16)
+    sum_common[...] = total[:7].reshape(sum_common.shape)
+    sum_side[...] = total[7:].reshape(sum_side.shape)
+    to_line = []
+    for k in (1, 2, 3):
+        copy = remote(
+            sum_common.at[toggled(line, k)], from_line.at[k - 1],
+            line_send.at[k - 1], line_recv.at[k - 1], on_line(k),
+        )
+        copy.start()
+        to_line.append(copy)
+    to_side = remote(sum_side.at[1 - side], from_side, side_send, side_recv, on_line(1))
+    to_side.start()
+
+    finish(1)
+    for copy in to_line:
+        copy.wait_recv()
+    to_side.wait_recv()
+    common = sum_common.shape[1]
+    total = sum_common[line].astype(jnp.float32)
+    for k in range(3):
+        total = total + from_line[k].astype(jnp.float32)
+    mine = gathered.at[core, member, line]
+    mine[:common] = total.astype(jnp.bfloat16)
+    total = sum_side[side].astype(jnp.float32) + from_side[...].astype(jnp.float32)
+    mine[common:] = total.astype(jnp.bfloat16)
+
+    along_line = []
+    for k in (1, 2, 3):
+        copy = remote(mine, mine, gline_send.at[k - 1], gline_recv.at[k - 1], on_line(k))
+        copy.start()
+        along_line.append(copy)
+    finish(2)
+    for copy in along_line:
+        copy.wait_recv()
+    quarter = gathered.at[core, member]
+    across_core = []
+    across_plane = []
+    for k in (1, 2, 3):
+        copy = remote(quarter, quarter, gplane_send.at[k - 1], gplane_recv.at[k - 1], on_plane(k))
+        copy.start()
+        across_plane.append(copy)
+    copy = remote(quarter, quarter, gcore_send.at[0], gcore_recv.at[0], core_mate)
+    copy.start()
+    across_core.append(copy)
+    finish(3)
+    for k in (1, 2, 3):
+        across_plane[k - 1].wait_recv()
+        piece = gathered.at[core, toggled(member, k)]
+        copy = remote(piece, piece, gcore_send.at[k], gcore_recv.at[k], core_mate)
+        copy.start()
+        across_core.append(copy)
+    for copy in across_core:
+        copy.wait_recv()
+    for copy in [to_core, to_side] + to_plane + to_line + along_line + across_plane + across_core:
+        copy.wait_send()
+
+    def sent(k):
+        swap_signal(k).wait_send()
+        swap_flow(k).wait_send()
+
+    each_chunk(sent)
+
+
+def fused(features, kernels, cotangent):
+    samples, band_rows, width, channels = features.shape
+    dilations = [span * band_rows for span in SPANS]
+    band = (band_rows, width, channels)
+    low, full = jnp.bfloat16, jnp.float32
+    half, quarter = channels // 2, channels // 4
+    common, sides = 7 * quarter // 4, 3 * quarter // 2
+    dma = pltpu.SemaphoreType.DMA
+    vmem = pltpu.VMEM
+    whole = pl.BlockSpec(memory_space=pltpu.VMEM)
+    result, grad_features, gathered = pl.pallas_call(
+        functools.partial(fused_kernel, dilations),
+        out_shape=(
+            jax.ShapeDtypeStruct(band, low),
+            jax.ShapeDtypeStruct(band, low),
+            jax.ShapeDtypeStruct((2, 4, 4, common + sides, half), low),
+        ),
+        in_specs=[whole, pl.BlockSpec(memory_space=pl.ANY), whole],
+        out_specs=(whole, whole, whole),
+        scratch_shapes=[
+            vmem((13 * channels, channels), low),
+            *[vmem(band, low) for _ in range(7)],
+            vmem(band, full),
+            vmem(band, full),
+            vmem((2, 4, 10, quarter, half), low),
+            vmem((4, 10, quarter, half), low),
+            vmem((4, 10, quarter, half), low),
+            vmem((3, 10, quarter, half), low),
+            vmem((4, common, half), low),
+            vmem((2, sides, half), low),
+            vmem((3, common, half), low),
+            vmem((sides, half), low),
+            dma((3,)),
+            dma((2 * CHUNKS,)),
+            dma((2 * CHUNKS,)),
+            dma, dma,
+            dma((3,)), dma((3,)),
+            dma((3,)), dma((3,)),
+            dma, dma,
+            dma((3,)), dma((3,)),
+            dma((3,)), dma((3,)),
+            dma((4,)), dma((4,)),
+        ],
+        compiler_params=pltpu.CompilerParams(
+            collective_id=0, has_side_effects=True, vmem_limit_bytes=48 * 2**20
+        ),
+        cost_estimate=pl.CostEstimate(
+            flops=48 * band_rows * width * channels * channels,
+            bytes_accessed=10 * band_rows * width * channels,
+            transcendentals=8 * band_rows * width * channels,
+        ),
+    )(
+        features.reshape(band),
+        kernels.reshape(27 * channels, channels),
+        cotangent.reshape(band),
+    )
+    cells = samples * band_rows * width * lax.axis_size("rows") * lax.axis_size("batch")
+    factor = 1.0 / math.sqrt(cells)
+    terms = gathered.astype(full) * factor
+    inner = terms[:, :, :, :common].reshape(2, 4, 7, quarter, half)
+    inner = jnp.transpose(inner, (2, 1, 3, 0, 4)).reshape(7, channels, channels)
+    outer = terms[:, :, :, common:].reshape(2, 4, 2, 3, quarter, half)
+    outer = jnp.transpose(outer, (2, 3, 1, 4, 0, 5)).reshape(2, 3, channels, channels)
+    first = jnp.stack([outer[1], inner[0:3], outer[0]])
+    second = jnp.pad(inner[3:6][None], ((1, 1), (0, 0), (0, 0), (0, 0)))
+    third = jnp.pad(inner[6:7][None], ((1, 1), (1, 1), (0, 0), (0, 0)))
+    return (
+        result.reshape(features.shape),
+        grad_features.reshape(features.shape),
+        jnp.stack([first, second, third]),
+    )
+
+
+def one_swap(features):
+    band_rows, width, channels = features.shape[1:]
+    dilations = [span * band_rows for span in SPANS]
+    return (
+        features.shape[0] == 1
+        and lax.axis_size("rows") == 2 * SPANS[0]
+        and lax.axis_size("batch") == 4
+        and SPANS[1] >= 2 * SPANS[0]
+        and dilations[1] < width <= dilations[2]
+        and band_rows % CHUNKS == 0
+        and channels == 256
+    )
+
+
+def device_part(features, kernels, cotangent):
+    if one_swap(features):
+        return fused(features, kernels, cotangent)
+    return local(features, kernels, cotangent)
+
+
 def solution(mesh):
     placed = (P("batch", "rows", None, None), P(), P("batch", "rows", None, None))
     return jax.shard_map(
-        local,
+        device_part,
         mesh=mesh,
         in_specs=placed,
         out_specs=(P("batch", "rows", None, None), P("batch", "rows", None, None), P()),

time: 218 us -> 103 us (0.47)
  waiting for transfers between devices: 156 us -> 0 us
  Pallas kernels: 0 us -> 76.1 us
  matrix products: 28.8 us -> 0 us
  local copies, waits for them, and re-layouts: 1.99 us -> 20.6 us
  between operations: 14.3 us -> 0.75 us
  other arithmetic: 12.3 us -> 4.12 us
  starting transfers between devices: 4.21 us -> 0 us
    psum x1 -> x0, waiting for transfers between devices: 116 us -> none  [local(): stacked = lax.psum(stacked, ('rows', 'batch'))]
    pallas_call x0 -> x1, Pallas kernels: none -> 76.1 us  [fused(): pl.pallas_call(functools.partial(fused_kernel, dilations), out_shape=(jax...]
    ppermute x2 -> x0, waiting for transfers between devices: 39.9 us -> none  [swapped(): lax.ppermute(value, axis, [(source, (source + steps) % count) for source...]
    dot_general x30 -> x0, matrix products: 28.8 us -> none  [the longest x10 12.4 us: tap_backward(): jnp.einsum('shwd,cd->shwc', source, kernel_row[column], preferred_element...]
    slice x0 -> x12, local copies, waits for them, and re-layouts: none -> 12.5 us  [the longest x7 10.2 us: fused(): first = jnp.stack([outer[1], inner[0:3], outer[0]])]
    ppermute x2 -> x0, starting transfers between devices: 4.17 us -> none  [swapped(): lax.ppermute(value, axis, [(source, (source + steps) % count) for source...]
    unnamed x10 -> x12, local copies, waits for them, and re-layouts: 0.22 us -> 3.68 us
    convert_element_type x4 -> x0, other arithmetic: 3.26 us -> none  [the longest x3 1.87 us: local(): grad_flow = (grad_flow.astype(jnp.float32) + dinput).astype(jnp.bfloat16)]
  transfers between devices with their start and end apart: 3 -> 0, of which waited for: 3 -> 0; matrix products, arithmetic and copies ran while one was open for 9% -> 0% of each run, Pallas kernels for 0% -> 0%
where the time goes in v2:
time: 103 us; the launch traced here: 102 us
  Pallas kernels  76.1 us (74%)
  local copies, waits for them, and re-layouts  20.6 us (20%)
  other arithmetic  4.12 us (4%)
    pallas_call x1, Pallas kernels, fused(): pl.pallas_call(functools.partial(fused_kernel, dilations), out_shape=(jax...  76.1 us
    slice x7, local copies, waits for them, and re-layouts, fused(): first = jnp.stack([outer[1], inner[0:3], outer[0]])  10.2 us
    another operation x2, other arithmetic, fused(): jnp.stack([first, second, third])  3.82 us
    unnamed x12, local copies, waits for them, and re-layouts  3.68 us

profile of v2, /device:TPU:0, one launch (start us, length us, event | category | flops | bytes accessed | tf_op | source)
XLA Modules:
  0.0 101.5 jit_solution(9959525131659732896)
XLA Ops:
  0.6 0.0 copy-start
  0.6 1.0 %copy-done = bf16[1,8,128,256]{3,2,1,0:T(8,128)(2,1)S(1)} copy-done((bf16[1,8,128,256]{3,2,1,0:T(8,128)(2,1)S(1)}, bf16[1,8,128,256]{3,2,1,0:T(8,128)(2,1)}, u32[]{:S(2)}) %copy-start) | copy-done | bytes 524312
  1.7 0.0 copy-start.1
  1.7 1.0 %copy-done.1 = bf16[1,8,128,256]{3,2,1,0:T(8,128)(2,1)S(1)} copy-done((bf16[1,8,128,256]{3,2,1,0:T(8,128)(2,1)S(1)}, bf16[1,8,128,256]{3,2,1,0:T(8,128)(2,1)}, u32[]{:S(2)}) %copy-start.1) | copy-done | bytes 524312
  2.7 76.1 %shard_map.58 = (bf16[8,128,256]{2,1,0:T(8,128)(2,1)S(1)}, bf16[8,128,256]{2,1,0:T(8,128)(2,1)S(1)}, bf16[2,4,4,208,128]{4,3,2,1,0:T(8,128)(2,1)S(1)}) custom-call(bf16[8,128,256]{2,1,0:T(8,128)(2,1)S(1)} %bitcast.19, bf16[6912,256]{1,0:T(8,128)(2,1)} %bitcast.24, bf16[8,128,256]{2,1,0:T(8,128)(2,1)S(1)} %bitcast.20), custom_call_target="tpu_custom_call" | custom-call | flops 3221225472 | bytes 2621440 | tf_op jit(solution)/shard_map/pallas_call | solution.py:457
  78.8 0.3 convert_multiply_fusion
  79.1 0.2 slice.39
  79.3 0.2 slice.41
  79.4 1.0 %fusion.1 = (f32[1,3,4,64,2,128]{5,3,1,0,2,4:T(8,128)S(1)}, f32[1,3,4,64,2,128]{5,3,1,0,2,4:T(8,128)}) fusion(f32[2,3,4,64,2,128]{5,3,1,0,2,4:T(8,128)S(1)} %bitcast.23), kind=kLoop, calls=%fused_computation.6 | loop fusion | bytes 3145728 | tf_op jit(solution)/shard_map/slice | solution.py:510
  80.5 1.5 %copy.6 = f32[1,3,4,64,2,128]{5,4,3,2,1,0:T(2,128)} copy(f32[1,3,4,64,2,128]{5,3,1,0,2,4:T(8,128)S(1)} %get-tuple-element.11) | data formatting | bytes 1572864 | tf_op jit(solution)/shard_map/slice | solution.py:510
  82.0 2.6 %slice.32 = f32[1,3,256,256]{3,2,1,0:T(8,128)} reshape(f32[1,3,4,64,2,128]{5,4,3,2,1,0:T(2,128)} %copy.6) | data formatting | bytes 1572864 | tf_op jit(solution)/shard_map/slice | solution.py:510
  84.6 1.0 %fusion = (f32[3,4,64,2,128]{4,2,0,1,3:T(8,128)S(1)}, f32[3,4,64,2,128]{4,2,0,1,3:T(8,128)}) fusion(f32[7,4,64,2,128]{4,2,0,1,3:T(8,128)S(1)} %bitcast.22), kind=kLoop, calls=%fused_computation.5 | loop fusion | bytes 3145728 | tf_op jit(solution)/shard_map/slice | solution.py:510
  85.7 0.6 copy.7
  86.3 0.6 stack.18
  86.9 0.0 copy-start.3
  87.0 0.2 copy.10
  87.2 0.9 broadcast_in_dim.7
  88.1 1.7 %copy.9 = f32[3,4,64,2,128]{4,3,2,1,0:T(2,128)S(1)} copy(f32[3,4,64,2,128]{4,2,0,1,3:T(8,128)} %get-tuple-element.10) | data formatting | bytes 1572864 | tf_op jit(solution)/shard_map/slice | solution.py:511
  89.8 1.5 %broadcast_in_dim.6 = f32[1,3,256,256]{3,2,1,0:T(8,128)} reshape(f32[3,4,64,2,128]{4,3,2,1,0:T(2,128)S(1)} %copy.9) | data formatting | bytes 1572864 | tf_op jit(solution)/shard_map/broadcast_in_dim | solution.py:511
  91.4 0.0 copy-done.3
  91.4 1.5 %copy.8 = f32[1,3,4,64,2,128]{5,4,3,2,1,0:T(2,128)} copy(f32[1,3,4,64,2,128]{5,3,1,0,2,4:T(8,128)S(1)} %copy-done.3) | data formatting | bytes 1572864 | tf_op jit(solution)/shard_map/slice | solution.py:510
  92.9 0.0 copy-start.2
  92.9 1.8 %slice.36 = f32[1,3,256,256]{3,2,1,0:T(8,128)S(1)} reshape(f32[1,3,4,64,2,128]{5,4,3,2,1,0:T(2,128)} %copy.8) | data formatting | bytes 1572864 | tf_op jit(solution)/shard_map/slice | solution.py:510
  94.7 0.0 copy-start.4
  94.7 1.4 %pad_bitcast_fusion.1 = f32[1,3,3,256,256]{4,3,2,1,0:T(8,128)S(1)} fusion(f32[1,3,256,256]{3,2,1,0:T(8,128)} %broadcast_in_dim.6), kind=kLoop, calls=%fused_computation.4 | loop fusion | bytes 3145728 | tf_op jit(solution)/shard_map/stack | solution.py:516
  96.1 0.0 copy-done.2
  96.1 0.0 copy-done.4
  96.1 0.4 maximum_bitcast_fusion
  96.5 3.4 %pad_maximum_fusion = f32[3,3,3,256,256]{4,3,2,1,0:T(8,128)} fusion(f32[1,3,3,256,256]{4,3,2,1,0:T(8,128)S(1)} %get-tuple-element.14, f32[1,3,3,256,256]{4,3,2,1,0:T(8,128)S(1)} %pad_bitcast_fusion.1, f32[1,3,3,256,256]{4,3,2,1,0:T(8,128)S(1)} %get-tuple-element.13), kind=kLoop, calls=%fused_computation | loop fusion | flops 3538944 | bytes 14155776 | tf_op jit(solution)/shard_map/stack | solution.py:516
  99.9 0.8 copy.13
  100.7 0.8 copy.14
  (1 shorter events, 0.0 us)
Async XLA Ops:
  0.6 1.0 %copy-start = (bf16[1,8,128,256]{3,2,1,0:T(8,128)(2,1)S(1)}, bf16[1,8,128,256]{3,2,1,0:T(8,128)(2,1)}, u32[]{:S(2)}) copy-start(bf16[1,8,128,256]{3,2,1,0:T(8,128)(2,1)} %param.3) | copy-start | bytes 1572868
  1.7 1.0 %copy-start.1 = (bf16[1,8,128,256]{3,2,1,0:T(8,128)(2,1)S(1)}, bf16[1,8,128,256]{3,2,1,0:T(8,128)(2,1)}, u32[]{:S(2)}) copy-start(bf16[1,8,128,256]{3,2,1,0:T(8,128)(2,1)} %param.5) | copy-start | bytes 1572868
  86.9 4.4 %copy-start.3 = (f32[1,3,4,64,2,128]{5,3,1,0,2,4:T(8,128)S(1)}, f32[1,3,4,64,2,128]{5,3,1,0,2,4:T(8,128)}, u32[]{:S(2)}) copy-start(f32[1,3,4,64,2,128]{5,3,1,0,2,4:T(8,128)} %get-tuple-element.12) | copy-start | bytes 2359300
  92.9 3.2 %copy-start.2 = (f32[1,3,256,256]{3,2,1,0:T(8,128)S(1)}, f32[1,3,256,256]{3,2,1,0:T(8,128)}, u32[]{:S(2)}) copy-start(f32[1,3,256,256]{3,2,1,0:T(8,128)} %slice.32) | copy-start | bytes 2359300
  94.7 1.4 %copy-start.4 = (f32[1,1,256,256]{3,2,1,0:T(8,128)S(1)}, f32[1,1,256,256]{3,2,1,0:T(8,128)}, u32[]{:S(2)}) copy-start(f32[1,1,256,256]{3,2,1,0:T(8,128)} %broadcast_in_dim.7) | copy-start | bytes 786436

commit v3 on v2

--- a/solution.py
+++ b/solution.py
@@ -442,6 +442,66 @@
         swap_flow(k).wait_send()
 
     each_chunk(sent)
+
+
+def spread_kernel(
+    factor, gathered, result, grad_features, out_result, out_features, out_kernels,
+    pieces, sems,
+):
+    copies = [
+        pltpu.make_async_copy(result, out_result, sems.at[0]),
+        pltpu.make_async_copy(grad_features, out_features, sems.at[1]),
+    ]
+    for copy in copies:
+        copy.start()
+    quarter, half = gathered.shape[3] * 4 // 13, gathered.shape[4]
+    common = 7 * quarter // 4
+    sides = 3 * quarter // 2
+    places = [None] * 13
+    for tap in range(3):
+        places[tap] = 3 + tap
+        places[3 + tap] = 12 + tap
+        places[7 + tap] = 6 + tap
+        places[10 + tap] = tap
+    places[6] = 22
+    blank = pieces.at[13:16]
+    blank[...] = jnp.zeros(blank.shape, jnp.float32)
+    zeros = [(9, 3), (15, 3), (18, 3), (21, 1), (23, 1), (24, 3)]
+    for slot, (tap, taps) in enumerate(zeros):
+        copies.append(
+            pltpu.make_async_copy(
+                blank.at[:taps], out_kernels.at[pl.ds(tap, taps)], sems.at[2 + slot]
+            )
+        )
+        copies[-1].start()
+    for tap in range(13):
+        for q in range(4):
+            done = 0
+            while done < quarter:
+                if tap < 7:
+                    spot, size = tap * quarter + done, common
+                    line, start = spot // size, spot % size
+                    offset = 0
+                else:
+                    upper, inner = (tap - 7) // 3, (tap - 7) % 3
+                    spot, size = inner * quarter + done, sides
+                    line, start = 2 * upper + spot // size, spot % size
+                    offset = common
+                rows = min(quarter - done, size - start)
+                for h in range(2):
+                    block = gathered[h, q, line, offset + start : offset + start + rows]
+                    pieces[
+                        tap,
+                        q * quarter + done : q * quarter + done + rows,
+                        h * half : (h + 1) * half,
+                    ] = block.astype(jnp.float32) * factor
+                done += rows
+        copies.append(
+            pltpu.make_async_copy(pieces.at[tap], out_kernels.at[places[tap]], sems.at[8 + tap])
+        )
+        copies[-1].start()
+    for copy in copies:
+        copy.wait()
 
 
 def fused(features, kernels, cotangent):
@@ -502,18 +562,23 @@
     )
     cells = samples * band_rows * width * lax.axis_size("rows") * lax.axis_size("batch")
     factor = 1.0 / math.sqrt(cells)
-    terms = gathered.astype(full) * factor
-    inner = terms[:, :, :, :common].reshape(2, 4, 7, quarter, half)
-    inner = jnp.transpose(inner, (2, 1, 3, 0, 4)).reshape(7, channels, channels)
-    outer = terms[:, :, :, common:].reshape(2, 4, 2, 3, quarter, half)
-    outer = jnp.transpose(outer, (2, 3, 1, 4, 0, 5)).reshape(2, 3, channels, channels)
-    first = jnp.stack([outer[1], inner[0:3], outer[0]])
-    second = jnp.pad(inner[3:6][None], ((1, 1), (0, 0), (0, 0), (0, 0)))
-    third = jnp.pad(inner[6:7][None], ((1, 1), (1, 1), (0, 0), (0, 0)))
+    anywhere = pl.BlockSpec(memory_space=pl.ANY)
+    result, grad_features, terms = pl.pallas_call(
+        functools.partial(spread_kernel, factor),
+        out_shape=(
+            jax.ShapeDtypeStruct(band, low),
+            jax.ShapeDtypeStruct(band, low),
+            jax.ShapeDtypeStruct((27, channels, channels), full),
+        ),
+        in_specs=[whole, anywhere, anywhere],
+        out_specs=(anywhere, anywhere, anywhere),
+        scratch_shapes=[vmem((16, channels, channels), full), dma((21,))],
+        compiler_params=pltpu.CompilerParams(vmem_limit_bytes=16 * 2**20),
+    )(gathered, result, grad_features)
     return (
         result.reshape(features.shape),
         grad_features.reshape(features.shape),
-        jnp.stack([first, second, third]),
+        terms.reshape(3, 3, 3, channels, channels),
     )
 
 

time: 103 us -> 83 us (0.81)
  local copies, waits for them, and re-layouts: 20.6 us -> 2.08 us
  other arithmetic: 4.12 us -> 0 us
  Pallas kernels: 76.1 us -> 79.4 us
    slice x12 -> x0, local copies, waits for them, and re-layouts: 12.5 us -> none  [the longest x7 10.2 us: fused(): first = jnp.stack([outer[1], inner[0:3], outer[0]])]
    another operation x2 -> x0, other arithmetic: 3.82 us -> none  [fused(): jnp.stack([first, second, third])]
    pallas_call x0 -> x1, Pallas kernels: none -> 3.38 us  [fused(): pl.pallas_call(functools.partial(spread_kernel, factor), out_shape=(jax.S...]
    broadcast_in_dim x2 -> x0, local copies, waits for them, and re-layouts: 2.44 us -> none  [the longest x1 1.53 us: fused(): second = jnp.pad(inner[3:6][None], ((1, 1), (0, 0), (0, 0), (0, 0)))]
    another operation x2 -> x0, local copies, waits for them, and re-layouts: 2 us -> none  [the longest x1 1.37 us: fused(): jnp.stack([first, second, third])]
    unnamed x12 -> x4, local copies, waits for them, and re-layouts: 3.68 us -> 2.08 us
where the time goes in v3:
time: 83 us; the launch traced here: 82.2 us
  Pallas kernels  79.4 us (96%)
  local copies, waits for them, and re-layouts  2.08 us (3%)
    pallas_call x1, Pallas kernels, fused(): pl.pallas_call(functools.partial(fused_kernel, dilations), out_shape=(jax...  76.1 us
    pallas_call x1, Pallas kernels, fused(): pl.pallas_call(functools.partial(spread_kernel, factor), out_shape=(jax.S...  3.38 us
    unnamed x4, local copies, waits for them, and re-layouts  2.08 us

profile of v3, /device:TPU:0, one launch (start us, length us, event | category | flops | bytes accessed | tf_op | source)
XLA Modules:
  0.0 82.2 jit_solution(2954908394646603488)
XLA Ops:
  0.6 0.0 copy-start
  0.6 1.0 %copy-done = bf16[1,8,128,256]{3,2,1,0:T(8,128)(2,1)S(1)} copy-done((bf16[1,8,128,256]{3,2,1,0:T(8,128)(2,1)S(1)}, bf16[1,8,128,256]{3,2,1,0:T(8,128)(2,1)}, u32[]{:S(2)}) %copy-start) | copy-done | bytes 524312
  1.7 0.0 copy-start.1
  1.7 1.0 %copy-done.1 = bf16[1,8,128,256]{3,2,1,0:T(8,128)(2,1)S(1)} copy-done((bf16[1,8,128,256]{3,2,1,0:T(8,128)(2,1)S(1)}, bf16[1,8,128,256]{3,2,1,0:T(8,128)(2,1)}, u32[]{:S(2)}) %copy-start.1) | copy-done | bytes 524312
  2.7 76.1 %shard_map.58 = (bf16[8,128,256]{2,1,0:T(8,128)(2,1)S(1)}, bf16[8,128,256]{2,1,0:T(8,128)(2,1)S(1)}, bf16[2,4,4,208,128]{4,3,2,1,0:T(8,128)(2,1)S(1)}) custom-call(bf16[8,128,256]{2,1,0:T(8,128)(2,1)S(1)} %bitcast.6, bf16[6912,256]{1,0:T(8,128)(2,1)} %bitcast.9, bf16[8,128,256]{2,1,0:T(8,128)(2,1)S(1)} %bitcast.7), custom_call_target="tpu_custom_call" | custom-call | flops 3221225472 | bytes 2621440 | tf_op jit(solution)/shard_map/pallas_call | solution.py:517
  78.8 3.4 %shard_map.59 = (bf16[8,128,256]{2,1,0:T(8,128)(2,1)}, bf16[8,128,256]{2,1,0:T(8,128)(2,1)}, f32[27,256,256]{2,1,0:T(8,128)}) custom-call(bf16[2,4,4,208,128]{4,3,2,1,0:T(8,128)(2,1)S(1)} %get-tuple-element.9.gathered, bf16[8,128,256]{2,1,0:T(8,128)(2,1)S(1)} %get-tuple-element.10.result, bf16[8,128,256]{2,1,0:T(8,128)(2,1)S(1)} %get-tuple-element.11.grad_features), custom_call_target="tpu_custom_call" | custom-call | tf_op jit(solution)/shard_map/pallas_call | solution.py:566
Async XLA Ops:
  0.6 1.0 %copy-start = (bf16[1,8,128,256]{3,2,1,0:T(8,128)(2,1)S(1)}, bf16[1,8,128,256]{3,2,1,0:T(8,128)(2,1)}, u32[]{:S(2)}) copy-start(bf16[1,8,128,256]{3,2,1,0:T(8,128)(2,1)} %param.3) | copy-start | bytes 1572868
  1.7 1.0 %copy-start.1 = (bf16[1,8,128,256]{3,2,1,0:T(8,128)(2,1)S(1)}, bf16[1,8,128,256]{3,2,1,0:T(8,128)(2,1)}, u32[]{:S(2)}) copy-start(bf16[1,8,128,256]{3,2,1,0:T(8,128)(2,1)} %param.5) | copy-start | bytes 1572868

commit v4 on v3

--- a/solution.py
+++ b/solution.py
@@ -142,6 +142,7 @@
 
 MESH = pl.DeviceIdType.MESH
 CHUNKS = 4
+FIRST_FLOWS, CORE_FLOWS, PLANE_FLOWS, LINE_FLOWS, LAST_FLOWS = ((0, 1), (2,), (), (), (3,))
 FLAT = (((1,), (0,)), ((), ()))
 TURNED = (((1,), (1,)), ((), ()))
 SUMMED = (((0,), (0,)), ((), ()))
@@ -296,10 +297,12 @@
     loads[1].wait()
     loads[2].wait()
 
-    def through(k):
+    def through(k, then=()):
         rows = pl.ds(k * step, step)
         shape = (step, width, channels)
         swap_signal(k).wait_recv()
+        for sent_now in then:
+            swap_flow(sent_now).start()
         upper = forward(other0[rows], (1 - lower) * 6, near)
         inner = (flat(center[rows]) + upper).astype(jnp.bfloat16).astype(jnp.float32)
         _, normed, gate = normalise(inner)
@@ -319,9 +322,13 @@
         dsignal = backward(flow, 9, mid)
         flow = flat(flow.astype(jnp.float32)) + activate_back(inner, dsignal)
         flow1[rows] = flow.astype(jnp.bfloat16).reshape(shape)
-        swap_flow(k).start()
-
-    each_chunk(through)
+
+    def run_through(k, carry):
+        through(k)
+        return carry
+
+    lax.fori_loop(0, CHUNKS - 1, run_through, 0)
+    through(CHUNKS - 1, FIRST_FLOWS)
 
     def keep(tap, terms):
         half, quarter = channels // 2, channels // 4
@@ -346,6 +353,8 @@
 
     to_core = remote(parts.at[1 - core], from_core, core_send, core_recv, core_mate)
     to_core.start()
+    for k in CORE_FLOWS:
+        swap_flow(k).start()
 
     def own_backward(k):
         rows = pl.ds(k * step, step)
@@ -373,6 +382,8 @@
         )
         copy.start()
         to_plane.append(copy)
+    for k in PLANE_FLOWS:
+        swap_flow(k).start()
 
     finish(0)
     for copy in to_plane:
@@ -393,6 +404,8 @@
         to_line.append(copy)
     to_side = remote(sum_side.at[1 - side], from_side, side_send, side_recv, on_line(1))
     to_side.start()
+    for k in LINE_FLOWS:
+        swap_flow(k).start()
 
     finish(1)
     for copy in to_line:
@@ -412,6 +425,8 @@
         copy = remote(mine, mine, gline_send.at[k - 1], gline_recv.at[k - 1], on_line(k))
         copy.start()
         along_line.append(copy)
+    for k in LAST_FLOWS:
+        swap_flow(k).start()
     finish(2)
     for copy in along_line:
         copy.wait_recv()

time: 83 us -> 74.3 us (0.90)
  Pallas kernels: 79.4 us -> 71.4 us
    pallas_call x1, Pallas kernels: 76.1 us -> 68 us  [fused(): pl.pallas_call(functools.partial(fused_kernel, dilations), out_shape=(jax...]
where the time goes in v4:
time: 74.3 us; the launch traced here: 74.1 us
  Pallas kernels  71.4 us (96%)
  local copies, waits for them, and re-layouts  2.08 us (3%)
    pallas_call x1, Pallas kernels, fused(): pl.pallas_call(functools.partial(fused_kernel, dilations), out_shape=(jax...  68 us
    pallas_call x1, Pallas kernels, fused(): pl.pallas_call(functools.partial(spread_kernel, factor), out_shape=(jax.S...  3.38 us
    unnamed x4, local copies, waits for them, and re-layouts  2.08 us

profile of v4, /device:TPU:0, one launch (start us, length us, event | category | flops | bytes accessed | tf_op | source)
XLA Modules:
  0.0 74.1 jit_solution(8681791442338842527)
XLA Ops:
  0.6 0.0 copy-start
  0.6 1.0 %copy-done = bf16[1,8,128,256]{3,2,1,0:T(8,128)(2,1)S(1)} copy-done((bf16[1,8,128,256]{3,2,1,0:T(8,128)(2,1)S(1)}, bf16[1,8,128,256]{3,2,1,0:T(8,128)(2,1)}, u32[]{:S(2)}) %copy-start) | copy-done | bytes 524312
  1.7 0.0 copy-start.1
  1.7 1.0 %copy-done.1 = bf16[1,8,128,256]{3,2,1,0:T(8,128)(2,1)S(1)} copy-done((bf16[1,8,128,256]{3,2,1,0:T(8,128)(2,1)S(1)}, bf16[1,8,128,256]{3,2,1,0:T(8,128)(2,1)}, u32[]{:S(2)}) %copy-start.1) | copy-done | bytes 524312
  2.7 68.0 %shard_map.58 = (bf16[8,128,256]{2,1,0:T(8,128)(2,1)S(1)}, bf16[8,128,256]{2,1,0:T(8,128)(2,1)S(1)}, bf16[2,4,4,208,128]{4,3,2,1,0:T(8,128)(2,1)S(1)}) custom-call(bf16[8,128,256]{2,1,0:T(8,128)(2,1)S(1)} %bitcast.6, bf16[6912,256]{1,0:T(8,128)(2,1)} %bitcast.9, bf16[8,128,256]{2,1,0:T(8,128)(2,1)S(1)} %bitcast.7), custom_call_target="tpu_custom_call" | custom-call | flops 3221225472 | bytes 2621440 | tf_op jit(solution)/shard_map/pallas_call | solution.py:532
  70.7 3.4 %shard_map.59 = (bf16[8,128,256]{2,1,0:T(8,128)(2,1)}, bf16[8,128,256]{2,1,0:T(8,128)(2,1)}, f32[27,256,256]{2,1,0:T(8,128)}) custom-call(bf16[2,4,4,208,128]{4,3,2,1,0:T(8,128)(2,1)S(1)} %get-tuple-element.9.gathered, bf16[8,128,256]{2,1,0:T(8,128)(2,1)S(1)} %get-tuple-element.10.result, bf16[8,128,256]{2,1,0:T(8,128)(2,1)S(1)} %get-tuple-element.11.grad_features), custom_call_target="tpu_custom_call" | custom-call | tf_op jit(solution)/shard_map/pallas_call | solution.py:581
Async XLA Ops:
  0.6 1.0 %copy-start = (bf16[1,8,128,256]{3,2,1,0:T(8,128)(2,1)S(1)}, bf16[1,8,128,256]{3,2,1,0:T(8,128)(2,1)}, u32[]{:S(2)}) copy-start(bf16[1,8,128,256]{3,2,1,0:T(8,128)(2,1)} %param.3) | copy-start | bytes 1572868
  1.7 1.0 %copy-start.1 = (bf16[1,8,128,256]{3,2,1,0:T(8,128)(2,1)S(1)}, bf16[1,8,128,256]{3,2,1,0:T(8,128)(2,1)}, u32[]{:S(2)}) copy-start(bf16[1,8,128,256]{3,2,1,0:T(8,128)(2,1)} %param.5) | copy-start | bytes 1572868
